TPU v7x, 32 devices: a whole 2x2x4 slice. The times are simulated.
32 devices in a mesh: row: 4 (over y, x), col: 8 (over z, core).
Axes of the slice: x: 2, y: 2, z: 4, core: 2. Of those that a mesh axis runs over, the one named last changes fastest.
Arguments:
- upper_tiles: bfloat16 [256, 5, 256, 256], P('row', None, 'col'), may hold values from -0.8984375 to 0.8984375
- occupied: int32 [256, 4], P(('row', 'col')), may hold values from 0 to 1, as said below
Outputs:
- square_tiles: bfloat16 [256, 5, 256, 256], P('row', None, 'col')
Inputs may be any that keep to these rules, and one draw needn't show every extreme that they name: Occupancy; its density differs between aligned groups of 8 block rows, and the diagonal block is always occupied (not listed).
All inputs are finite; a program needn't handle non-finite values.
Results may differ from a plain program's by a relative error of at most 0.0024.
Values may be sent and summed in bfloat16 or wider, within the bound.
A program may use at most 256 MiB of HBM per device.

v0:
```python
import functools

import jax
import jax.numpy as jnp
from jax import lax
from jax.experimental import pallas as pl
from jax.experimental.pallas import tpu as pltpu
from jax.sharding import PartitionSpec as P

MESH = pl.DeviceIdType.MESH


def band_square_kernel(
    rows_n,
    cols_n,
    width,
    up,
    occ,
    out,
    tiles,
    strip,
    prod,
    occ_v,
    kept,
    in_send,
    in_recv,
    halo_send,
    halo_recv,
    out_send,
    out_recv,
    occ_sem,
    loc_sem,
):
    block_rows, block = tiles.shape[0], tiles.shape[2]
    slab = block // cols_n
    row, col = lax.axis_index("row"), lax.axis_index("col")
    odd = lax.rem(row, 2)

    def turned(c):
        return jnp.where(odd == 1, cols_n - 1 - c, c)

    pos = turned(col)
    chunk = row * cols_n + pos
    step = 1 - 2 * odd
    has_next, has_prev = chunk < rows_n * cols_n - 1, chunk > 0
    next_out, prev_out = pos == cols_n - 1, pos == 0
    next_dev = (jnp.where(next_out, row + 1, row), jnp.where(next_out, col, col + step))
    prev_dev = (jnp.where(prev_out, row - 1, row), jnp.where(prev_out, col, col - step))

    def other(k):
        return lax.rem(col + k, cols_n)

    barrier = pltpu.get_barrier_semaphore()

    @pl.loop(1, cols_n)
    def _(k):
        pl.semaphore_signal(barrier, inc=1, device_id=(row, other(k)), device_id_type=MESH)

    @pl.when(next_out & has_next)
    def _():
        pl.semaphore_signal(barrier, inc=1, device_id=next_dev, device_id_type=MESH)

    @pl.when(prev_out & has_prev)
    def _():
        pl.semaphore_signal(barrier, inc=1, device_id=prev_dev, device_id_type=MESH)

    outside = (next_out & has_next) | (prev_out & has_prev)
    pl.semaphore_wait(barrier, cols_n - 1 + jnp.where(outside, 1, 0))

    def slab_of(c):
        return pl.ds(pl.multiple_of(c * slab, slab), slab)

    def cells(stage):
        for r in range(block_rows):
            cut = width - r if r < width else block_rows - r
            first, rest = (0, cut), (cut, width + 1)
            if r >= width:
                first, rest = rest, first
            if stage == 0:
                yield r, first
            elif (stage == 1) == (r <= width):
                yield r, rest

    def piece_of(stage, c):
        count = sum(hi - lo for _, (lo, hi) in cells(stage))
        deep = max(n for n in range(1, width + 2) if count % n == 0 and count // n <= block_rows)
        return tiles.at[: count // deep, :deep, slab_of(c), :]

    mine = slab_of(col)
    def send(stage):
        for r, (lo, hi) in cells(stage):
            pltpu.make_async_copy(
                up.at[pos * block_rows + r, lo:hi], tiles.at[r, lo:hi, mine, :], loc_sem.at[stage]
            ).start()

            @pl.loop(1, cols_n)
            def _(k):
                dst = other(k)
                pltpu.make_async_remote_copy(
                    src_ref=up.at[turned(dst) * block_rows + r, lo:hi],
                    dst_ref=tiles.at[r, lo:hi, mine, :],
                    send_sem=in_send.at[dst],
                    recv_sem=in_recv.at[stage, col],
                    device_id=(row, dst),
                    device_id_type=MESH,
                ).start()

    send(0)
    send(1)

    partner = cols_n - 1 - col
    occ_copy = pltpu.make_async_remote_copy(
        src_ref=occ,
        dst_ref=occ_v,
        send_sem=occ_sem.at[0],
        recv_sem=occ_sem.at[1],
        device_id=(row, partner),
        device_id_type=MESH,
    )

    @pl.when(odd == 1)
    def _():
        occ_copy.start()
        occ_copy.wait()

    @pl.when(odd == 0)
    def _():
        here = pltpu.make_async_copy(occ, occ_v, occ_sem.at[1])
        here.start()
        here.wait()

    shape = occ_v.shape
    index = (
        chunk * block_rows
        + lax.broadcasted_iota(jnp.int32, shape, 0)
        + lax.broadcasted_iota(jnp.int32, shape, 1)
        + 1
    )
    total = rows_n * cols_n * block_rows
    kept[...] = jnp.where((occ_v[...] == 1) & (index < total), 1, 0)

    def part_of(n):
        return slice(n * block, (n + 1) * block)

    @pl.when(jnp.logical_not(has_prev))
    def _():
        for q in range(width):
            strip[q, :, : (width - q) * block] = jnp.zeros(
                (block, (width - q) * block), strip.dtype
            )

    @pl.when(jnp.logical_not(has_next))
    def _():
        for m in range(width):
            strip[block_rows + m, :, width * block : (2 * width - m) * block] = jnp.zeros(
                (block, (width - m) * block), strip.dtype
            )

    def arrive(stage):
        piece = piece_of(stage, col)
        pltpu.make_async_copy(piece, piece, loc_sem.at[stage]).wait()

        @pl.loop(1, cols_n)
        def _(k):
            src = other(k)
            piece = piece_of(stage, src)
            pltpu.make_async_copy(piece, piece, in_recv.at[stage, src]).wait()

    def place(stage):
        for d in range(width + 1):
            if stage == 0:
                lo, hi = block_rows - d, block_rows - d + width
            elif stage == 1:
                lo, hi = width - d, min(width + 1, block_rows - d)
            else:
                lo, hi = width + 1, block_rows - d
            if lo >= hi:
                continue

            @pl.loop(lo, hi)
            def _(j):
                r = lax.rem(j, block_rows)
                tile = tiles[r, d]
                if d == 0:
                    full = tile.astype(jnp.float32)
                    strip[r, :, part_of(width)] = (0.5 * (full + full.T)).astype(strip.dtype)
                else:
                    flag = kept[pl.ds(r, 1), :][:, d - 1 : d]
                    tile = jnp.where(flag == 1, tile, jnp.zeros_like(tile))
                    strip[r, :, part_of(width + d)] = tile
                    strip[r + d, :, part_of(width - d)] = tile.T

    def halo(way, m):
        if way == 0:
            cut = slice(0, (width - m) * block)
            src, dst, dev = block_rows + m, m, next_dev
        else:
            cut = slice(width * block, (2 * width - m) * block)
            src, dst, dev = m, block_rows + m, prev_dev
        return pltpu.make_async_remote_copy(
            src_ref=strip.at[src, :, cut],
            dst_ref=strip.at[dst, :, cut],
            send_sem=halo_send.at[way, m],
            recv_sem=halo_recv.at[way, m],
            device_id=dev,
            device_id_type=MESH,
        )

    arrive(0)
    send(2)
    place(0)

    @pl.when(has_next)
    def _():
        for m in range(width):
            halo(0, m).start()

    @pl.when(has_prev)
    def _():
        for m in range(width):
            halo(1, m).start()

    arrive(1)
    place(1)

    @pl.when(has_prev)
    def _():
        for m in range(width):
            halo(0, m).wait_recv()

    def products(r):
        flags = kept[pl.ds(r, 1), :]
        for e in range(width + 1):
            value = lax.dot_general(
                strip[r, :, e * block :],
                strip[r + e, :, : (2 * width + 1 - e) * block],
                (((1,), (1,)), ((), ())),
                preferred_element_type=jnp.float32,
            )
            if e > 0:
                value = jnp.where(flags[:, e - 1 : e] == 1, value, 0.0)
            prod[r, e] = value.astype(prod.dtype)
        place_row = pos * block_rows + r
        pltpu.make_async_copy(prod.at[r, :, mine, :], out.at[place_row], loc_sem.at[3]).start()

        @pl.loop(1, cols_n)
        def _(k):
            dst = other(k)
            pltpu.make_async_remote_copy(
                src_ref=prod.at[r, :, slab_of(dst), :],
                dst_ref=out.at[place_row],
                send_sem=out_send.at[dst],
                recv_sem=out_recv.at[col],
                device_id=(row, dst),
                device_id_type=MESH,
            ).start()

    products(0)
    arrive(2)
    place(2)

    @pl.when(has_next)
    def _():
        for m in range(width):
            halo(1, m).wait_recv()

    for d in range(1, width):

        @pl.loop(block_rows, block_rows + width - d)
        def _(r):
            strip[r + d, :, part_of(width - d)] = strip[r, :, part_of(width + d)].T

    pl.loop(1, block_rows)(products)

    @pl.when(has_next)
    def _():
        for m in range(width):
            halo(0, m).wait_send()

    @pl.when(has_prev)
    def _():
        for m in range(width):
            halo(1, m).wait_send()

    def rows_of(c):
        return pl.ds(turned(c) * block_rows, block_rows)

    whole = out.at[rows_of(col)]
    pltpu.make_async_copy(whole, whole, loc_sem.at[3]).wait()

    @pl.loop(1, cols_n)
    def _(k):
        dev = other(k)
        sent = up.at[rows_of(dev)]
        pltpu.make_async_copy(sent, sent, in_send.at[dev]).wait()
        left = prod.at[:, :, slab_of(dev), :]
        pltpu.make_async_copy(left, left, out_send.at[dev]).wait()
        came = out.at[rows_of(dev)]
        pltpu.make_async_copy(came, came, out_recv.at[dev]).wait()


def shards(rows_n, cols_n, upper_tiles, occupied):
    block_rows, width = occupied.shape
    block = upper_tiles.shape[3]
    flags = jnp.pad(occupied, ((0, 0), (0, 128 - width)))
    dma = pltpu.SemaphoreType.DMA
    return pl.pallas_call(
        functools.partial(band_square_kernel, rows_n, cols_n, width),
        out_shape=jax.ShapeDtypeStruct(upper_tiles.shape, upper_tiles.dtype),
        in_specs=[pl.BlockSpec(memory_space=pl.ANY)] * 2,
        out_specs=pl.BlockSpec(memory_space=pl.ANY),
        scratch_shapes=[
            pltpu.VMEM((block_rows, width + 1, block, block), jnp.bfloat16),
            pltpu.VMEM((block_rows + width, block, (2 * width + 1) * block), jnp.bfloat16),
            pltpu.VMEM((block_rows, width + 1, block, block), jnp.bfloat16),
            pltpu.VMEM((block_rows, 128), jnp.int32),
            pltpu.VMEM((block_rows, 128), jnp.int32),
            dma((cols_n,)),
            dma((3, cols_n)),
            dma((2, width)),
            dma((2, width)),
            dma((cols_n,)),
            dma((cols_n,)),
            dma((2,)),
            dma((4,)),
        ],
        compiler_params=pltpu.CompilerParams(
            collective_id=0, has_side_effects=True, vmem_limit_bytes=48 * 2**20
        ),
        cost_estimate=pl.CostEstimate(
            flops=2 * 35 * block_rows * block**3, bytes_accessed=2 * upper_tiles.size * 2, transcendentals=0
        ),
    )(upper_tiles, flags)


def solution(mesh):
    return jax.shard_map(
        functools.partial(shards, mesh.shape["row"], mesh.shape["col"]),
        mesh=mesh,
        in_specs=(P("row", None, "col", None), P(("row", "col"), None)),
        out_specs=P("row", None, "col", None),
        check_vma=False,
    )
```

profile of v0, /device:TPU:11, one launch (start us, length us, event | category | flops | bytes accessed | tf_op | source)
XLA Modules:
  0.0 249.9 jit_solution(17984612722456672062)
XLA Ops:
  0.0 0.8 copy.3
  0.8 246.7 %shard_map.28 = bf16[64,5,32,256]{3,2,1,0:T(8,128)(2,1)S(1)} custom-call(bf16[64,5,32,256]{3,2,1,0:T(8,128)(2,1)} %up.1, s32[8,128]{1,0:T(8,128)S(1)} %pad.4.occ), custom_call_target="tpu_custom_call" | custom-call | flops 9395240960 | bytes 10485760 | tf_op jit(solution)/shard_map/pallas_call | solution.py:307
  247.5 2.4 copy.5
  (1 shorter events, 0.0 us)
where the time goes:
time: 250 us
  Pallas kernels  247 us (99%)
  local copies, waits for them, and re-layouts  3.12 us (1%)
    pallas_call x1, Pallas kernels, shards(): pl.pallas_call(functools.partial(band_square_kernel, rows_n, cols_n, widt...  247 us

commit v1 on v0

--- a/solution.py
+++ b/solution.py
@@ -20,12 +20,17 @@
     tiles,
     strip,
     prod,
-    occ_v,
+    edge,
+    occ_here,
+    occ_far,
     kept,
+    kept_far,
     in_send,
     in_recv,
     halo_send,
     halo_recv,
+    edge_send,
+    edge_recv,
     out_send,
     out_recv,
     occ_sem,
@@ -42,7 +47,9 @@
     pos = turned(col)
     chunk = row * cols_n + pos
     step = 1 - 2 * odd
+    lower, upper = cols_n // 2 - 1, cols_n // 2
     has_next, has_prev = chunk < rows_n * cols_n - 1, chunk > 0
+    pass_next, pass_prev = has_next & (pos != lower), has_prev & (pos != upper)
     next_out, prev_out = pos == cols_n - 1, pos == 0
     next_dev = (jnp.where(next_out, row + 1, row), jnp.where(next_out, col, col + step))
     prev_dev = (jnp.where(prev_out, row - 1, row), jnp.where(prev_out, col, col - step))
@@ -105,39 +112,73 @@
                     device_id_type=MESH,
                 ).start()
 
+    def edge_span(way, m):
+        return (lower * block_rows + width + m, width - m, m + 1) if way == 0 else (
+            upper * block_rows + m, 0, width - m)
+
+    edge_to = (turned(upper), turned(lower))
+
+    def send_edge(way):
+        for m in range(width):
+            r, lo, count = edge_span(way, m)
+            src, dst = up.at[r, lo : lo + count], edge.at[m, :count, mine, :]
+
+            @pl.when(col != edge_to[way])
+            def _():
+                pltpu.make_async_remote_copy(
+                    src_ref=src,
+                    dst_ref=dst,
+                    send_sem=edge_send.at[way],
+                    recv_sem=edge_recv.at[col],
+                    device_id=(row, edge_to[way]),
+                    device_id_type=MESH,
+                ).start()
+
+            @pl.when(col == edge_to[way])
+            def _():
+                pltpu.make_async_copy(src, dst, edge_recv.at[col]).start()
+
+    def edge_piece(c):
+        return tiles.at[: width // 2, : width + 1, slab_of(c), :]
+
+    def arrive_edge():
+        @pl.loop(0, cols_n)
+        def _(c):
+            piece = edge_piece(c)
+            pltpu.make_async_copy(piece, piece, edge_recv.at[c]).wait()
+
     send(0)
+    send_edge(0)
+    send_edge(1)
     send(1)
 
     partner = cols_n - 1 - col
     occ_copy = pltpu.make_async_remote_copy(
         src_ref=occ,
-        dst_ref=occ_v,
+        dst_ref=occ_far,
         send_sem=occ_sem.at[0],
         recv_sem=occ_sem.at[1],
         device_id=(row, partner),
         device_id_type=MESH,
     )
-
-    @pl.when(odd == 1)
-    def _():
-        occ_copy.start()
-        occ_copy.wait()
-
-    @pl.when(odd == 0)
-    def _():
-        here = pltpu.make_async_copy(occ, occ_v, occ_sem.at[1])
-        here.start()
-        here.wait()
-
-    shape = occ_v.shape
-    index = (
-        chunk * block_rows
-        + lax.broadcasted_iota(jnp.int32, shape, 0)
-        + lax.broadcasted_iota(jnp.int32, shape, 1)
-        + 1
+    occ_copy.start()
+    occ_local = pltpu.make_async_copy(occ, occ_here, occ_sem.at[2])
+    occ_local.start()
+    occ_local.wait()
+    occ_copy.wait()
+
+    shape = kept.shape
+    offset = (
+        lax.broadcasted_iota(jnp.int32, shape, 0) + lax.broadcasted_iota(jnp.int32, shape, 1) + 1
     )
     total = rows_n * cols_n * block_rows
-    kept[...] = jnp.where((occ_v[...] == 1) & (index < total), 1, 0)
+    chunk_far = row * cols_n + cols_n - 1 - pos
+    flags_here, flags_far = occ_here[...], occ_far[...]
+    for ref, flags, number in (
+        (kept, jnp.where(odd == 1, flags_far, flags_here), chunk),
+        (kept_far, jnp.where(odd == 1, flags_here, flags_far), chunk_far),
+    ):
+        ref[...] = jnp.where((flags == 1) & (number * block_rows + offset < total), 1, 0)
 
     def part_of(n):
         return slice(n * block, (n + 1) * block)
@@ -182,13 +223,32 @@
                 r = lax.rem(j, block_rows)
                 tile = tiles[r, d]
                 if d == 0:
-                    full = tile.astype(jnp.float32)
-                    strip[r, :, part_of(width)] = (0.5 * (full + full.T)).astype(strip.dtype)
+                    strip[r, :, part_of(width)] = symmetric(tile)
                 else:
-                    flag = kept[pl.ds(r, 1), :][:, d - 1 : d]
-                    tile = jnp.where(flag == 1, tile, jnp.zeros_like(tile))
+                    tile = masked(tile, kept[pl.ds(r, 1), :], d)
                     strip[r, :, part_of(width + d)] = tile
                     strip[r + d, :, part_of(width - d)] = tile.T
+
+    def masked(tile, flags, d):
+        return jnp.where(flags[:, d - 1 : d] == 1, tile, jnp.zeros_like(tile))
+
+    def symmetric(tile):
+        full = tile.astype(jnp.float32)
+        return (0.5 * (full + full.T)).astype(strip.dtype)
+
+    def place_upper():
+        for m in range(width):
+            for q in range(m + 1):
+                flags = kept_far[width + m : width + m + 1, :]
+                tile = masked(edge[m, q], flags, width - m + q)
+                strip[q, :, part_of(m - q)] = tile.T
+
+    def place_lower():
+        for m in range(width):
+            strip[block_rows + m, :, part_of(width)] = symmetric(edge[m, 0])
+            for d in range(1, width - m):
+                flags = kept_far[m : m + 1, :]
+                strip[block_rows + m, :, part_of(width + d)] = masked(edge[m, d], flags, d)
 
     def halo(way, m):
         if way == 0:
@@ -210,12 +270,12 @@
     send(2)
     place(0)
 
-    @pl.when(has_next)
+    @pl.when(pass_next)
     def _():
         for m in range(width):
             halo(0, m).start()
 
-    @pl.when(has_prev)
+    @pl.when(pass_prev)
     def _():
         for m in range(width):
             halo(1, m).start()
@@ -223,10 +283,15 @@
     arrive(1)
     place(1)
 
-    @pl.when(has_prev)
+    @pl.when(pass_prev)
     def _():
         for m in range(width):
             halo(0, m).wait_recv()
+
+    @pl.when(pos == upper)
+    def _():
+        arrive_edge()
+        place_upper()
 
     def products(r):
         flags = kept[pl.ds(r, 1), :]
@@ -259,10 +324,15 @@
     arrive(2)
     place(2)
 
-    @pl.when(has_next)
+    @pl.when(pass_next)
     def _():
         for m in range(width):
             halo(1, m).wait_recv()
+
+    @pl.when(pos == lower)
+    def _():
+        arrive_edge()
+        place_lower()
 
     for d in range(1, width):
 
@@ -272,15 +342,22 @@
 
     pl.loop(1, block_rows)(products)
 
-    @pl.when(has_next)
+    @pl.when(pass_next)
     def _():
         for m in range(width):
             halo(0, m).wait_send()
 
-    @pl.when(has_prev)
+    @pl.when(pass_prev)
     def _():
         for m in range(width):
             halo(1, m).wait_send()
+
+    for way in range(2):
+
+        @pl.when(col != edge_to[way])
+        def _():
+            piece = edge_piece(col)
+            pltpu.make_async_copy(piece, piece, edge_send.at[way]).wait()
 
     def rows_of(c):
         return pl.ds(turned(c) * block_rows, block_rows)
@@ -313,15 +390,20 @@
             pltpu.VMEM((block_rows, width + 1, block, block), jnp.bfloat16),
             pltpu.VMEM((block_rows + width, block, (2 * width + 1) * block), jnp.bfloat16),
             pltpu.VMEM((block_rows, width + 1, block, block), jnp.bfloat16),
+            pltpu.VMEM((width, width, block, block), jnp.bfloat16),
+            pltpu.VMEM((block_rows, 128), jnp.int32),
+            pltpu.VMEM((block_rows, 128), jnp.int32),
             pltpu.VMEM((block_rows, 128), jnp.int32),
             pltpu.VMEM((block_rows, 128), jnp.int32),
             dma((cols_n,)),
             dma((3, cols_n)),
             dma((2, width)),
             dma((2, width)),
+            dma((2,)),
             dma((cols_n,)),
             dma((cols_n,)),
-            dma((2,)),
+            dma((cols_n,)),
+            dma((3,)),
             dma((4,)),
         ],
         compiler_params=pltpu.CompilerParams(

time: 250 us -> 244 us (0.976)
  Pallas kernels: 247 us -> 240 us
    pallas_call x1, Pallas kernels: 247 us -> 240 us  [shards(): pl.pallas_call(functools.partial(band_square_kernel, rows_n, cols_n, widt...]
where the time goes in v1:
time: 244 us; the launch traced here: 243 us
  Pallas kernels  240 us (98%)
  local copies, waits for them, and re-layouts  3.12 us (1%)
    pallas_call x1, Pallas kernels, shards(): pl.pallas_call(functools.partial(band_square_kernel, rows_n, cols_n, widt...  240 us

profile of v1, /device:TPU:11, one launch (start us, length us, event | category | flops | bytes accessed | tf_op | source)
XLA Modules:
  0.0 243.2 jit_solution(14623893361900251893)
XLA Ops:
  0.0 0.8 copy.3
  0.8 240.0 %shard_map.28 = bf16[64,5,32,256]{3,2,1,0:T(8,128)(2,1)S(1)} custom-call(bf16[64,5,32,256]{3,2,1,0:T(8,128)(2,1)} %up.1, s32[8,128]{1,0:T(8,128)S(1)} %pad.4.occ), custom_call_target="tpu_custom_call" | custom-call | flops 9395240960 | bytes 10485760 | tf_op jit(solution)/shard_map/pallas_call | solution.py:384
  240.8 2.4 copy.5
  (1 shorter events, 0.0 us)

commit v2 on v1

--- a/solution.py
+++ b/solution.py
@@ -57,6 +57,13 @@
     def other(k):
         return lax.rem(col + k, cols_n)
 
+    half = cols_n // 2
+    inside, base = lax.rem(col, half), col // half * half
+
+    def target(k):
+        step = jnp.where(k < half, k, k - half + 1)
+        return jnp.where(k < half, half - base, base) + lax.rem(inside + step, half)
+
     barrier = pltpu.get_barrier_semaphore()
 
     @pl.loop(1, cols_n)
@@ -100,9 +107,9 @@
                 up.at[pos * block_rows + r, lo:hi], tiles.at[r, lo:hi, mine, :], loc_sem.at[stage]
             ).start()
 
-            @pl.loop(1, cols_n)
+            @pl.loop(0, cols_n - 1)
             def _(k):
-                dst = other(k)
+                dst = target(k)
                 pltpu.make_async_remote_copy(
                     src_ref=up.at[turned(dst) * block_rows + r, lo:hi],
                     dst_ref=tiles.at[r, lo:hi, mine, :],
@@ -308,9 +315,9 @@
         place_row = pos * block_rows + r
         pltpu.make_async_copy(prod.at[r, :, mine, :], out.at[place_row], loc_sem.at[3]).start()
 
-        @pl.loop(1, cols_n)
+        @pl.loop(0, cols_n - 1)
         def _(k):
-            dst = other(k)
+            dst = target(k)
             pltpu.make_async_remote_copy(
                 src_ref=prod.at[r, :, slab_of(dst), :],
                 dst_ref=out.at[place_row],

time: 244 us -> 246 us (level)
  no operation moved by 1% of the time
where the time goes in v2:
time: 246 us; the launch traced here: 243 us
  Pallas kernels  240 us (98%)
  local copies, waits for them, and re-layouts  3.12 us (1%)
    pallas_call x1, Pallas kernels, shards(): pl.pallas_call(functools.partial(band_square_kernel, rows_n, cols_n, widt...  240 us

profile of v2, /device:TPU:11, one launch (start us, length us, event | category | flops | bytes accessed | tf_op | source)
XLA Modules:
  0.0 243.2 jit_solution(268094292201283412)
XLA Ops:
  0.0 0.8 copy.3
  0.8 240.1 %shard_map.28 = bf16[64,5,32,256]{3,2,1,0:T(8,128)(2,1)S(1)} custom-call(bf16[64,5,32,256]{3,2,1,0:T(8,128)(2,1)} %up.1, s32[8,128]{1,0:T(8,128)S(1)} %pad.4.occ), custom_call_target="tpu_custom_call" | custom-call | flops 9395240960 | bytes 10485760 | tf_op jit(solution)/shard_map/pallas_call | solution.py:391
  240.8 2.4 copy.5
  (1 shorter events, 0.0 us)
